TPU v7x, 768 devices: a whole 4x8x12 slice. The times are simulated.
768 devices in a mesh: batch: 16 (over z_hi, x), feat: 48 (over y, z_lo, core).
Axes of the slice: x: 4, y: 8, z: 12 (z_hi: 4, z_lo: 3; z = z_hi * 3 + z_lo), core: 2. Of those that a mesh axis runs over, the one named last changes fastest.
Arguments:
- view_a: bfloat16 [2048, 6144], P('batch', 'feat'), may hold values from -6 to 6
- view_b: bfloat16 [2048, 6144], P('batch', 'feat'), may hold values from -6 to 6
- weight_off: float32 [], replicated, may hold values from 0.05 to 0.2
- loss_grad: float32 [], replicated, may hold values from 0.5 to 2
Outputs:
- grad_a: float32 [2048, 6144], P('batch', 'feat')
- grad_b: float32 [2048, 6144], P('batch', 'feat')
All inputs are finite; a program needn't handle non-finite values.
Results may differ from a plain program's by a relative error of at most 0.0012.
Values may be sent and summed in bfloat16 or wider, within the bound.
A program may use at most 32 MiB of HBM per device.

v0:
```python
import jax
import jax.numpy as jnp
from jax import lax
from jax.sharding import PartitionSpec as P


def weight_tile(corr, weight_off, row_first):
    row_ids = lax.broadcasted_iota(jnp.int32, corr.shape, 0) + row_first
    col_ids = lax.broadcasted_iota(jnp.int32, corr.shape, 1)
    return jnp.where(row_ids == col_ids, -2.0 * (1.0 - corr), 2.0 * weight_off * corr)


def local(view_a, view_b, weight_off, loss_grad):
    row_count, block_width = view_a.shape
    image_count = row_count * lax.axis_size("batch")
    row_first = lax.axis_index("feat") * block_width
    whole_b = lax.all_gather(view_b, "feat", axis=1, tiled=True)
    corr_part = (
        lax.dot_general(
            view_a, whole_b, (((0,), (0,)), ((), ())), preferred_element_type=jnp.float32
        )
        / image_count
    )
    corr = lax.psum(corr_part, "batch")
    weights = weight_tile(corr, weight_off, row_first)
    grad_a = lax.dot_general(
        whole_b.astype(jnp.float32),
        weights,
        (((1,), (1,)), ((), ())),
        precision=lax.Precision.HIGHEST,
        preferred_element_type=jnp.float32,
    )
    first_block = view_a.astype(jnp.float32)
    summed = lax.psum_scatter(
        lax.dot_general(
            weights,
            first_block,
            (((0,), (1,)), ((), ())),
            precision=lax.Precision.HIGHEST,
            preferred_element_type=jnp.float32,
        ),
        "feat",
        scatter_dimension=0,
        tiled=True,
    )
    grad_b = loss_grad * summed.T
    return (loss_grad * grad_a, grad_b)


def solution(mesh):
    return jax.shard_map(
        local,
        mesh=mesh,
        in_specs=(P("batch", "feat"), P("batch", "feat"), P(), P()),
        out_specs=(P("batch", "feat"), P("batch", "feat")),
        check_vma=False,
    )
```

profile of v0, /device:TPU:192, one launch (start us, length us, event | category | flops | bytes accessed | tf_op | source)
XLA Modules:
  0.0 700.0 jit_solution(13426263047113566291)
XLA Ops:
  7.2 0.0 copy-start
  7.2 0.0 all-gather.2.cloned.1.call-start
  7.2 0.7 all-gather.2.cloned.1.call-update
  7.9 0.0 all-reduce.2.cloned.1.call-start
  8.0 175.2 %all-gather.2.cloned.1.call-done = bf16[128,6144]{1,0:T(8,128)(2,1)} async-done(((bf16[128,128]{1,0:T(8,128)(2,1)}), bf16[128,6144]{1,0:T(8,128)(2,1)}) %all-gather.2.cloned.1.call-update) | async-done | bytes 1572880 | tf_op jit(solution)/shard_map/all_gather | solution.py:17
  183.1 0.0 copy-done
  183.1 3.7 convolution_multiply_fusion
  186.8 0.0 all-reduce.2.cloned.1.call-update
  186.8 0.0 reduce-scatter.2.cloned.1.call-start
  187.5 254.5 %all-reduce.2.cloned.1.call-done = f32[128,6144]{1,0:T(8,128)} async-done(((f32[128,6144]{1,0:T(8,128)}), f32[128,6144]{1,0:T(8,128)}) %all-reduce.2.cloned.1.call-update) | async-done | bytes 3145744 | tf_op jit(solution)/shard_map/psum | solution.py:24
  442.1 6.4 fusion
  448.5 0.0 copy-start.1
  448.5 0.0 reduce-scatter.2.cloned.1.call-update
  449.4 1.1 copy-done.1
  450.4 3.6 fusion.11
  454.0 0.7 copy.6
  454.7 237.2 %reduce-scatter.2.cloned.1.call-done = f32[128,128]{1,0:T(8,128)} async-done(((f32[6144,128]{1,0:T(8,128)}), f32[128,128]{1,0:T(8,128)}) %reduce-scatter.2.cloned.1.call-update) | async-done | bytes 65552 | tf_op jit(solution)/shard_map/reduce_scatter | solution.py:34
  691.9 0.8 multiply_bitcast_fusion
  692.8 0.7 copy.7
  (1 shorter events, 0.0 us)
Async XLA Ops:
  7.2 176.0 %copy-start = (bf16[128,128]{1,0:T(8,128)(2,1)S(1)}, bf16[128,128]{1,0:T(8,128)(2,1)}, u32[]{:S(2)}) copy-start(bf16[128,128]{1,0:T(8,128)(2,1)} %param.4) | copy-start | bytes 98308
  7.2 176.0 %all-gather.2.cloned.1.call-start = ((), (), s32[]{:S(2)}) async-start(), calls=%async_computation.1 | async-start | bytes 1605632 | tf_op jit(solution)/shard_map/all_gather | solution.py:17
  7.9 434.2 %all-reduce.2.cloned.1.call-start = ((), (), s32[]{:S(2)}) async-start(), calls=%async_computation.2 | async-start | bytes 6291456 | tf_op jit(solution)/shard_map/psum | solution.py:24
  186.8 505.1 %reduce-scatter.2.cloned.1.call-start = ((), (), s32[]{:S(2)}) async-start(), calls=%async_computation.3 | async-start | bytes 3211264 | tf_op jit(solution)/shard_map/reduce_scatter | solution.py:34
  448.5 1.9 copy-start.1
Sparse Core Ops, SparseCore 0:
  10.3 172.7 all-gather.1
  187.0 255.0 all-reduce.1
  448.7 243.1 reduce-scatter.1
where the time goes:
time: 700 us
  waiting for transfers between devices  668 us (95%)
  between operations  15.2 us (2%)
  matrix products  13.7 us (2%)
    psum x1, waiting for transfers between devices, local(): corr = lax.psum(corr_part, 'batch')  255 us
    reduce_scatter x1, waiting for transfers between devices, local(): lax.psum_scatter(lax.dot_general(weights, first_block, (((0,), (1,)), (()...  237 us
    all_gather x1, waiting for transfers between devices, local(): whole_b = lax.all_gather(view_b, 'feat', axis=1, tiled=True)  175 us
  transfers between devices with their start and end apart: 3, of which 3 were waited for; matrix products, arithmetic and copies ran while one was open for 1% of the time, Pallas kernels for 0%

commit v1 on v0

v1 whole, which is shorter than its diff:
```python
import jax
import jax.numpy as jnp
from jax import lax
from jax.sharding import PartitionSpec as P


def local(view_a, view_b, weight_off, loss_grad):
    rows, width = view_a.shape
    images = rows * lax.axis_size("batch")
    own = jnp.stack([view_a, view_b])
    cols = lax.all_gather(own, "batch", axis=1, tiled=True)
    gram_part = lax.dot_general(
        own, cols, (((2,), (2,)), ((0,), (0,))), preferred_element_type=jnp.float32
    )
    gram = lax.psum(gram_part, "feat")
    diag = jnp.sum(cols[0].astype(jnp.float32) * cols[1].astype(jnp.float32), axis=0) / images
    shift = -2.0 + 2.0 * (1.0 - weight_off) * diag
    rounded = lax.reduce_precision(gram, 8, 7)
    high = rounded.astype(jnp.bfloat16)
    low = (gram - rounded).astype(jnp.bfloat16)

    def apply(which, other):
        out = jnp.dot(high[which], cols[other], preferred_element_type=jnp.float32)
        return out + jnp.dot(low[which], cols[other], preferred_element_type=jnp.float32)

    scale = 2.0 * weight_off / images
    grad_a = loss_grad * (scale * apply(1, 0) + view_b.astype(jnp.float32) * shift)
    grad_b = loss_grad * (scale * apply(0, 1) + view_a.astype(jnp.float32) * shift)
    return grad_a, grad_b


def solution(mesh):
    return jax.shard_map(
        local,
        mesh=mesh,
        in_specs=(P("batch", "feat"), P("batch", "feat"), P(), P()),
        out_specs=(P("batch", "feat"), P("batch", "feat")),
        check_vma=False,
    )
```

time: 700 us -> 530 us (0.76)
  waiting for transfers between devices: 668 us -> 505 us
  matrix products: 13.7 us -> 5.54 us
    reduce_scatter x1 -> x0, waiting for transfers between devices: 237 us -> none  [local(): lax.psum_scatter(lax.dot_general(weights, first_block, (((0,), (1,)), (()...]
    psum x1, waiting for transfers between devices: 255 us -> 428 us  [local(): gram = lax.psum(gram_part, 'feat')]
    all_gather x1, waiting for transfers between devices: 175 us -> 77.5 us  [local(): cols = lax.all_gather(own, 'batch', axis=1, tiled=True)]
    dot_general x3 -> x5, matrix products: 13.7 us -> 5.54 us  [the longest x1 3.09 us: local(): lax.dot_general(own, cols, (((2,), (2,)), ((0,), (0,))), preferred_elemen...]
  transfers between devices with their start and end apart: 3 -> 2, of which waited for: 3 -> 2; matrix products, arithmetic and copies ran while one was open for 1% -> 0% of each run, Pallas kernels for 0% -> 0%
where the time goes in v1:
time: 530 us
  waiting for transfers between devices  505 us (95%)
  between operations  15.4 us (3%)
  matrix products  5.54 us (1%)
    psum x1, waiting for transfers between devices, local(): gram = lax.psum(gram_part, 'feat')  428 us
    all_gather x1, waiting for transfers between devices, local(): cols = lax.all_gather(own, 'batch', axis=1, tiled=True)  77.5 us
  transfers between devices with their start and end apart: 2, of which 2 were waited for; matrix products, arithmetic and copies ran while one was open for 0% of the time, Pallas kernels for 0%

profile of v1, /device:TPU:192, one launch (start us, length us, event | category | flops | bytes accessed | tf_op | source)
XLA Modules:
  0.0 530.0 jit_solution(17012432564557450296)
XLA Ops:
  7.2 0.0 all-gather.2.cloned.1.call-start
  7.2 1.4 pad_maximum_fusion
  8.6 0.0 all-gather.2.cloned.1.call-update
  8.6 0.0 all-reduce.2.cloned.1.call-start
  8.7 77.5 %all-gather.2.cloned.1.call-done = bf16[2,2048,128]{2,1,0:T(8,128)(2,1)} async-done(((bf16[2,128,128]{2,1,0:T(8,128)(2,1)}), bf16[2,2048,128]{2,1,0:T(8,128)(2,1)}) %all-gather.2.cloned.1.call-update) | async-done | bytes 1048592 | tf_op jit(solution)/shard_map/all_gather | solution.py:11
  86.2 0.0 copy-start
  86.2 3.1 fusion.9
  89.3 0.0 all-reduce.2.cloned.1.call-update
  90.6 0.0 copy-done
  90.6 0.3 multiply_reduce_fusion
  90.9 427.6 %all-reduce.2.cloned.1.call-done = f32[2,128,2048]{2,1,0:T(8,128)} async-done(((f32[2,128,2048]{2,1,0:T(8,128)}), f32[2,128,2048]{2,1,0:T(8,128)}) %all-reduce.2.cloned.1.call-update) | async-done | bytes 2097168 | tf_op jit(solution)/shard_map/psum | solution.py:15
  518.5 2.0 fusion
  520.5 0.0 copy-start.1
  520.5 0.0 copy-start.2
  520.5 0.3 fusion.7
  520.8 0.3 fusion.8
  521.1 0.1 copy-done.1
  521.3 0.9 fusion.3
  522.2 0.0 copy-done.2
  522.2 0.9 fusion.6
  (1 shorter events, 0.0 us)
Async XLA Ops:
  7.2 79.0 %all-gather.2.cloned.1.call-start = ((), (), s32[]{:S(2)}) async-start(), calls=%async_computation | async-start | bytes 1114112 | tf_op jit(solution)/shard_map/all_gather | solution.py:11
  8.6 509.9 %all-reduce.2.cloned.1.call-start = ((), (), s32[]{:S(2)}) async-start(), calls=%async_computation.1 | async-start | bytes 4194304 | tf_op jit(solution)/shard_map/psum | solution.py:15
  86.2 4.4 copy-start
  520.5 0.8 copy-start.1
  520.5 1.7 copy-start.2
Sparse Core Ops, SparseCore 0:
  12.2 73.9 all-gather.1
  89.4 429.0 all-reduce.1

commit v2 on v1

v2 whole, which is shorter than its diff:
```python
import functools

import jax
import jax.numpy as jnp
from jax import lax
from jax.experimental import pallas as pl
from jax.experimental.pallas import tpu as pltpu
from jax.sharding import PartitionSpec as P

MESH = pl.DeviceIdType.MESH
NX, NY, NHI, NLO = 4, 8, 4, 3
NZ = NHI * NLO
T = 128
J = 48
JR = NX * J
PY = JR // NY
HOPS = ((6, 5), (5, 6))


def dev(x, y, z, c):
    return ((z // NLO) * NX + x, (y * NLO + z % NLO) * 2 + c)


def kernel(
    images,
    w_ref,
    l_ref,
    a_ref,
    b_ref,
    ga_ref,
    gb_ref,
    own,
    xbuf,
    xj,
    part,
    rsb,
    red,
    gt,
    op,
    rx,
    fsum,
    fin,
    dgs,
    dgx,
    dgs2,
    dgz,
    ssem,
    p1r,
    sibr,
    p2r,
    rsr,
    agr,
    p4r,
    p5r,
    dxr,
    dzr,
):
    bi = lax.axis_index("batch")
    fi = lax.axis_index("feat")
    zh, x = bi // NX, bi % NX
    y, zl, c = fi // (NLO * 2), (fi // 2) % NLO, fi % 2
    z = zh * NLO + zl
    zr, zf = (z + 1) % NZ, (z + NZ - 1) % NZ

    def at_z(k):
        return (z + k + 2 * NZ) % NZ

    peers = [dev(x, y, zn, t) for zn in (zr, zf) for t in range(2)]
    peers += [dev(x, y, z, 1 - c)]
    peers += [dev((x + d) % NX, y, z, c) for d in range(1, NX)]
    peers += [dev(x, (y + d) % NY, z, t) for d in range(1, NY) for t in range(2)]
    peers += [dev(x, y, zh * NLO + (zl + d) % NLO, t) for d in range(1, NLO) for t in range(2)]
    peers += [dev(x, y, (z + NLO * d) % NZ, c) for d in range(1, NHI)]
    bar = pltpu.get_barrier_semaphore()
    for p in peers:
        pl.semaphore_signal(bar, inc=1, device_id=p, device_id_type=MESH)
    own[0] = a_ref[...]
    own[1] = b_ref[...]
    prod = a_ref[...].astype(jnp.float32) * b_ref[...].astype(jnp.float32)
    dgs[...] = jnp.sum(prod.reshape(T // 8, 8, T), axis=0)
    xbuf[z, c] = own[c]
    pl.semaphore_wait(bar, len(peers))

    sent = []

    def copy(src, dst, rsem, target):
        cp = pltpu.make_async_remote_copy(
            src_ref=src,
            dst_ref=dst,
            send_sem=ssem.at[len(sent)],
            recv_sem=rsem,
            device_id=target,
            device_id_type=MESH,
        )
        sent.append(cp)
        cp.start()

    def arrived(dst, rsem):
        pltpu.make_async_remote_copy(
            src_ref=dst,
            dst_ref=dst,
            send_sem=ssem.at[0],
            recv_sem=rsem,
            device_id=dev(x, y, z, 1 - c),
            device_id_type=MESH,
        ).wait_recv()

    for t in range(2):
        copy(own.at[t], xbuf.at[z, c], p1r.at[0, 0, c], dev(x, y, zr, t))
        copy(own.at[t], xbuf.at[z, c], p1r.at[1, 0, c], dev(x, y, zf, t))
    copy(own.at[1 - c], xbuf.at[z, c], sibr.at[0], dev(x, y, z, 1 - c))
    for d in range(1, NX):
        copy(dgs, dgx.at[d - 1], dxr.at[d - 1], dev((x + d) % NX, y, z, c))

    near = jnp.where(zl == 2, 1, NHI - 1)
    group = [zh, (zh + near) % NHI, (zh + NHI - near) % NHI, (zh + 2) % NHI]
    first = jnp.where(zl == 2, T - J, zl * J)
    first = pl.multiple_of(first, 16)

    def send_j():
        xj[:, :, x] = xbuf[pl.ds(zh * NLO, NLO), :, pl.ds(first, J), :]
        for d in (2, 1, 3):
            x1 = (x + d) % NX
            copy(
                xbuf.at[pl.ds(zh * NLO, NLO), :, pl.ds(first, J), :],
                xj.at[:, :, x],
                p2r.at[d - 1],
                dev(x1, y, z, c),
            )

    def wait_j():
        for d in (1, 3, 2):
            arrived(xj.at[:, :, (x + NX - d) % NX], p2r.at[d - 1])

    def gram(k):
        acc = jnp.zeros((JR, T), jnp.float32)
        for i in range(NLO):
            for j in range(2):
                acc += lax.dot_general(
                    xj[i, j].reshape(JR, T),
                    xbuf[group[k] * NLO + i, j],
                    (((1,), (1,)), ((), ())),
                    preferred_element_type=jnp.float32,
                )
        part[k] = acc
        for d in (4, 3, 5, 2, 6, 1, 7):
            y1 = (y + d) % NY
            copy(
                part.at[k, pl.ds(pl.multiple_of(y1 * PY, 8), PY), :],
                rsb.at[k, d - 1],
                rsr.at[k, d - 1],
                dev(x, y1, z, c),
            )

    def reduce(k):
        tot = part[k, pl.ds(pl.multiple_of(y * PY, 8), PY), :]
        for d in (1, 7, 2, 6, 3, 5, 4):
            arrived(rsb.at[k, d - 1], rsr.at[k, d - 1])
            tot += rsb[k, d - 1]
        red[k] = tot
        for d in (4, 3, 5, 2, 6, 1, 7, 0):
            copy(
                red.at[k],
                gt.at[k, pl.ds(pl.multiple_of(y * PY, 8), PY), :],
                agr.at[k, d],
                dev(x, (y + d) % NY, z, 1 - c),
            )

    for s in range(6):
        for j in range(2):
            for r in range(2):
                if s >= HOPS[r][j]:
                    continue
                zc = at_z(-1 - s) if r == 0 else at_z(1 + s)
                arrived(xbuf.at[zc, j], p1r.at[r, s, j])
                if s + 1 < HOPS[r][j]:
                    copy(
                        xbuf.at[zc, j],
                        xbuf.at[zc, j],
                        p1r.at[r, s + 1, j],
                        dev(x, y, zr if r == 0 else zf, c),
                    )
        if s == 0:
            arrived(xbuf.at[z, 1 - c], sibr.at[0])
        if s == 1:
            send_j()
        if s == 2:
            tot = dgs[...]
            for d in range(1, NX):
                arrived(dgx.at[d - 1], dxr.at[d - 1])
                tot += dgx[d - 1]
            dgs2[...] = tot
            for d in range(1, NHI):
                copy(dgs2, dgz.at[d - 1], dzr.at[d - 1], dev(x, y, (z + NLO * d) % NZ, c))
            wait_j()
            gram(0)
        if s == 3:
            gram(1)
        if s == 4:
            gram(2)
            reduce(0)
    gram(3)
    reduce(1)
    reduce(2)
    reduce(3)

    for k in range(NHI):
        for d in range(NY):
            y1 = (y + NY - d) % NY
            arrived(gt.at[k, pl.ds(pl.multiple_of(y1 * PY, 8), PY), :], agr.at[k, d])
        g = gt[k]
        high = g.astype(jnp.bfloat16)
        low = (g - high.astype(jnp.float32)).astype(jnp.bfloat16)
        for f in range(NLO * 2):
            tile = xbuf[group[k] * NLO + f // 2, f % 2]
            new = jnp.dot(high, tile, preferred_element_type=jnp.float32)
            new += jnp.dot(low, tile, preferred_element_type=jnp.float32)
            new = new.reshape(NX, J, T)
            op[f] = new if k == 0 else op[f] + new
    for d in (2, 1, 3):
        x1 = (x + d) % NX
        copy(op.at[:, x1], rx.at[d - 1], p4r.at[d - 1], dev(x1, y, z, c))
    total = op[:, x]
    for d in (1, 3, 2):
        arrived(rx.at[d - 1], p4r.at[d - 1])
        total += rx[d - 1]
    fsum[...] = total

    fin[c, zl] = fsum[zl * 2 + c]
    hops = [(d, e) for d in range(NLO) for e in range(2) if d or e]
    for d, e in hops:
        zl1, c1 = (zl + d) % NLO, (c + e) % 2
        copy(fsum.at[zl1 * 2 + c1], fin.at[c, zl], p5r.at[d, e], dev(x, y, zh * NLO + zl1, c1))
    tot = dgs2[...]
    for d in range(1, NHI):
        arrived(dgz.at[d - 1], dzr.at[d - 1])
        tot += dgz[d - 1]
    weight_off = w_ref[0]
    loss_grad = l_ref[0]
    shift = -2.0 + (2.0 * (1.0 - weight_off) / images) * jnp.sum(tot, axis=0, keepdims=True)
    scale = 2.0 * weight_off / images
    for d, e in hops:
        arrived(fin.at[(c + e) % 2, (zl + NLO - d) % NLO], p5r.at[d, e])
    for t, (out, other) in enumerate(((ga_ref, b_ref), (gb_ref, a_ref))):
        for i, rows in enumerate((J, J, T - 2 * J)):
            at = pl.ds(i * J, rows)
            gram_term = fin[t, i, pl.ds(J - rows, rows), :]
            out[at, :] = loss_grad * (scale * gram_term + other[at, :].astype(jnp.float32) * shift)
    for cp in sent:
        cp.wait_send()


def local(view_a, view_b, weight_off, loss_grad):
    images = view_a.shape[0] * lax.axis_size("batch")
    f32, bf16 = jnp.float32, jnp.bfloat16
    dma = pltpu.SemaphoreType.DMA
    vmem = pl.BlockSpec(memory_space=pltpu.VMEM)
    smem = pl.BlockSpec(memory_space=pltpu.SMEM)
    return pl.pallas_call(
        functools.partial(kernel, float(images)),
        out_shape=[jax.ShapeDtypeStruct((T, T), f32)] * 2,
        in_specs=[smem, smem, vmem, vmem],
        out_specs=[vmem, vmem],
        scratch_shapes=[
            pltpu.VMEM((2, T, T), bf16),
            pltpu.VMEM((NZ, 2, T, T), bf16),
            pltpu.VMEM((NLO, 2, NX, J, T), bf16),
            pltpu.VMEM((NHI, JR, T), f32),
            pltpu.VMEM((NHI, NY - 1, PY, T), f32),
            pltpu.VMEM((NHI, PY, T), f32),
            pltpu.VMEM((NHI, JR, T), f32),
            pltpu.VMEM((NLO * 2, NX, J, T), f32),
            pltpu.VMEM((NX - 1, NLO * 2, J, T), f32),
            pltpu.VMEM((NLO * 2, J, T), f32),
            pltpu.VMEM((2, NLO, J, T), f32),
            pltpu.VMEM((8, T), f32),
            pltpu.VMEM((NX - 1, 8, T), f32),
            pltpu.VMEM((8, T), f32),
            pltpu.VMEM((NHI - 1, 8, T), f32),
            dma((104,)),
            dma((2, 6, 2)),
            dma((1,)),
            dma((NX - 1,)),
            dma((NHI, NY - 1)),
            dma((NHI, NY)),
            dma((NX - 1,)),
            dma((NLO, 2)),
            dma((NX - 1,)),
            dma((NHI - 1,)),
        ],
        compiler_params=pltpu.CompilerParams(
            collective_id=0, has_side_effects=True, vmem_limit_bytes=32 << 20
        ),
        name="gram_grads",
    )(weight_off.reshape(1), loss_grad.reshape(1), view_a, view_b)


def solution(mesh):
    return jax.shard_map(
        local,
        mesh=mesh,
        in_specs=(P("batch", "feat"), P("batch", "feat"), P(), P()),
        out_specs=(P("batch", "feat"), P("batch", "feat")),
        check_vma=False,
    )
```

time: 530 us -> 70.4 us (0.13)
  the two profiles are of different devices: /device:TPU:192 before, /device:TPU:3 now
where the time goes in v2:
time: 70.4 us; the launch traced here: 70.1 us
  Pallas kernels  65.4 us (93%)
  local copies, waits for them, and re-layouts  2.77 us (4%)
  between operations  1.94 us (3%)
    pallas_call x1, Pallas kernels, local(): pl.pallas_call(functools.partial(kernel, float(images)), out_shape=[jax.S...  65.4 us
    unnamed x6, local copies, waits for them, and re-layouts  2.77 us

profile of v2, /device:TPU:3, one launch (start us, length us, event | category | flops | bytes accessed | tf_op | source)
XLA Modules:
  0.0 70.1 jit_solution(2907578125234487832)
XLA Ops:
  1.9 0.0 copy-start
  1.9 0.7 %copy-done = bf16[128,128]{1,0:T(8,128)(2,1)S(1)} copy-done((bf16[128,128]{1,0:T(8,128)(2,1)S(1)}, bf16[128,128]{1,0:T(8,128)(2,1)}, u32[]{:S(2)}) %copy-start) | copy-done | bytes 32792
  2.7 0.0 copy-start.1
  2.7 0.8 %copy-done.1 = bf16[128,128]{1,0:T(8,128)(2,1)S(1)} copy-done((bf16[128,128]{1,0:T(8,128)(2,1)S(1)}, bf16[128,128]{1,0:T(8,128)(2,1)}, u32[]{:S(2)}) %copy-start.1) | copy-done | bytes 32792
  3.4 65.4 %gram_grads.1 = (f32[128,128]{1,0:T(8,128)S(1)}, f32[128,128]{1,0:T(8,128)S(1)}) custom-call(f32[1]{0:T(128)} %bitcast.2.w_ref, f32[1]{0:T(128)} %bitcast.3.l_ref, bf16[128,128]{1,0:T(8,128)(2,1)S(1)} %copy-done, bf16[128,128]{1,0:T(8,128)(2,1)S(1)} %copy-done.1), custom_call_target="tpu_custom_call" | custom-call | tf_op jit(solution)/shard_map/gram_grads/pallas_call | solution.py:259
  68.8 0.6 copy.10
  69.4 0.6 copy.11
Async XLA Ops:
  1.9 0.8 %copy-start = (bf16[128,128]{1,0:T(8,128)(2,1)S(1)}, bf16[128,128]{1,0:T(8,128)(2,1)}, u32[]{:S(2)}) copy-start(bf16[128,128]{1,0:T(8,128)(2,1)} %a_ref.1) | copy-start | bytes 98308
  2.7 0.8 %copy-start.1 = (bf16[128,128]{1,0:T(8,128)(2,1)S(1)}, bf16[128,128]{1,0:T(8,128)(2,1)}, u32[]{:S(2)}) copy-start(bf16[128,128]{1,0:T(8,128)(2,1)} %b_ref.1) | copy-start | bytes 98308

commit v3 on v2

--- a/solution.py
+++ b/solution.py
@@ -14,7 +14,9 @@
 J = 48
 JR = NX * J
 PY = JR // NY
-HOPS = ((6, 5), (5, 6))
+TREE = {2: 0, -2: 0, 1: 0, -1: 0, 4: 2, -4: -2, 3: 2, -3: -2, 5: 4, -5: -4, 6: 4}
+NEXT = {p: [d for d in TREE if TREE[d] == p] for p in (0, *TREE)}
+FAR = max(abs(d) for d in NEXT[0])
 
 
 def dev(x, y, z, c):
@@ -45,6 +47,9 @@
     dgs2,
     dgz,
     ssem,
+    loaded,
+    xin,
+    yin,
     p1r,
     sibr,
     p2r,
@@ -60,24 +65,26 @@
     zh, x = bi // NX, bi % NX
     y, zl, c = fi // (NLO * 2), (fi // 2) % NLO, fi % 2
     z = zh * NLO + zl
-    zr, zf = (z + 1) % NZ, (z + NZ - 1) % NZ
 
     def at_z(k):
         return (z + k + 2 * NZ) % NZ
 
-    peers = [dev(x, y, zn, t) for zn in (zr, zf) for t in range(2)]
-    peers += [dev(x, y, z, 1 - c)]
-    peers += [dev((x + d) % NX, y, z, c) for d in range(1, NX)]
-    peers += [dev(x, (y + d) % NY, z, t) for d in range(1, NY) for t in range(2)]
-    peers += [dev(x, y, zh * NLO + (zl + d) % NLO, t) for d in range(1, NLO) for t in range(2)]
-    peers += [dev(x, y, (z + NLO * d) % NZ, c) for d in range(1, NHI)]
+    yr, yl = (y + 1) % NY, (y + NY - 1) % NY
+    xr, xl = (x + 1) % NX, (x + NX - 1) % NX
     bar = pltpu.get_barrier_semaphore()
+    peers = [dev(x, y, z, 1 - c)]
+    peers += [dev(x, yn, z, t) for yn in (yr, yl) for t in range(2)]
+    peers += [dev(xn, y, z, c) for xn in (xr, xl)]
+    peers += [dev(x, y, at_z(s * d), t) for d in range(1, FAR + 1) for s in (1, -1) for t in range(2)]
     for p in peers:
         pl.semaphore_signal(bar, inc=1, device_id=p, device_id_type=MESH)
-    own[0] = a_ref[...]
-    own[1] = b_ref[...]
-    prod = a_ref[...].astype(jnp.float32) * b_ref[...].astype(jnp.float32)
-    dgs[...] = jnp.sum(prod.reshape(T // 8, 8, T), axis=0)
+    loads = [
+        pltpu.make_async_copy(ref, own.at[t], loaded.at[t]) for t, ref in enumerate((a_ref, b_ref))
+    ]
+    for cp in loads:
+        cp.start()
+    for cp in loads:
+        cp.wait()
     xbuf[z, c] = own[c]
     pl.semaphore_wait(bar, len(peers))
 
@@ -105,10 +112,21 @@
             device_id_type=MESH,
         ).wait_recv()
 
+    sign = 1 - 2 * c
     for t in range(2):
-        copy(own.at[t], xbuf.at[z, c], p1r.at[0, 0, c], dev(x, y, zr, t))
-        copy(own.at[t], xbuf.at[z, c], p1r.at[1, 0, c], dev(x, y, zf, t))
-    copy(own.at[1 - c], xbuf.at[z, c], sibr.at[0], dev(x, y, z, 1 - c))
+        for d in NEXT[0]:
+            copy(own.at[t], xbuf.at[z, c], p1r.at[c, d + 5], dev(x, y, at_z(sign * d), t))
+        if t == 0:
+            pl.semaphore_signal(xin, inc=1, device_id=dev(xl, y, z, c), device_id_type=MESH)
+            copy(own.at[1 - c], xbuf.at[z, c], sibr.at[0], dev(x, y, z, 1 - c))
+    for n in range(NY // 2 - 1):
+        for i, yn in enumerate((yr, yl)):
+            pl.semaphore_signal(yin.at[n, i], inc=1, device_id=dev(x, yn, z, c), device_id_type=MESH)
+        for i in range(2):
+            pl.semaphore_wait(yin.at[n, i], 1)
+    pl.semaphore_wait(xin, 1)
+    first_view, second_view = own[0].astype(jnp.float32), own[1].astype(jnp.float32)
+    dgs[...] = jnp.sum((first_view * second_view).reshape(T // 8, 8, T), axis=0)
     for d in range(1, NX):
         copy(dgs, dgx.at[d - 1], dxr.at[d - 1], dev((x + d) % NX, y, z, c))
 
@@ -166,43 +184,32 @@
                 dev(x, (y + d) % NY, z, 1 - c),
             )
 
-    for s in range(6):
+    for d in TREE:
         for j in range(2):
-            for r in range(2):
-                if s >= HOPS[r][j]:
-                    continue
-                zc = at_z(-1 - s) if r == 0 else at_z(1 + s)
-                arrived(xbuf.at[zc, j], p1r.at[r, s, j])
-                if s + 1 < HOPS[r][j]:
-                    copy(
-                        xbuf.at[zc, j],
-                        xbuf.at[zc, j],
-                        p1r.at[r, s + 1, j],
-                        dev(x, y, zr if r == 0 else zf, c),
-                    )
-        if s == 0:
+            s = 1 - 2 * j
+            zc = at_z(-s * d)
+            arrived(xbuf.at[zc, j], p1r.at[j, d + 5])
+            for e in NEXT[d]:
+                copy(xbuf.at[zc, j], xbuf.at[zc, j], p1r.at[j, e + 5], dev(x, y, at_z(s * (e - d)), c))
+        if d == -1:
             arrived(xbuf.at[z, 1 - c], sibr.at[0])
-        if s == 1:
             send_j()
-        if s == 2:
-            tot = dgs[...]
-            for d in range(1, NX):
-                arrived(dgx.at[d - 1], dxr.at[d - 1])
-                tot += dgx[d - 1]
-            dgs2[...] = tot
-            for d in range(1, NHI):
-                copy(dgs2, dgz.at[d - 1], dzr.at[d - 1], dev(x, y, (z + NLO * d) % NZ, c))
+        if d == -3:
             wait_j()
             gram(0)
-        if s == 3:
             gram(1)
-        if s == 4:
+        if d == -5:
             gram(2)
-            reduce(0)
     gram(3)
-    reduce(1)
-    reduce(2)
-    reduce(3)
+    tot = dgs[...]
+    for d in range(1, NX):
+        arrived(dgx.at[d - 1], dxr.at[d - 1])
+        tot += dgx[d - 1]
+    dgs2[...] = tot
+    for d in range(1, NHI):
+        copy(dgs2, dgz.at[d - 1], dzr.at[d - 1], dev(x, y, (z + NLO * d) % NZ, c))
+    for k in range(NHI):
+        reduce(k)
 
     for k in range(NHI):
         for d in range(NY):
@@ -211,26 +218,32 @@
         g = gt[k]
         high = g.astype(jnp.bfloat16)
         low = (g - high.astype(jnp.float32)).astype(jnp.bfloat16)
-        for f in range(NLO * 2):
-            tile = xbuf[group[k] * NLO + f // 2, f % 2]
-            new = jnp.dot(high, tile, preferred_element_type=jnp.float32)
-            new += jnp.dot(low, tile, preferred_element_type=jnp.float32)
-            new = new.reshape(NX, J, T)
-            op[f] = new if k == 0 else op[f] + new
-    for d in (2, 1, 3):
-        x1 = (x + d) % NX
-        copy(op.at[:, x1], rx.at[d - 1], p4r.at[d - 1], dev(x1, y, z, c))
-    total = op[:, x]
-    for d in (1, 3, 2):
-        arrived(rx.at[d - 1], p4r.at[d - 1])
-        total += rx[d - 1]
-    fsum[...] = total
-
-    fin[c, zl] = fsum[zl * 2 + c]
-    hops = [(d, e) for d in range(NLO) for e in range(2) if d or e]
-    for d, e in hops:
-        zl1, c1 = (zl + d) % NLO, (c + e) % 2
-        copy(fsum.at[zl1 * 2 + c1], fin.at[c, zl], p5r.at[d, e], dev(x, y, zh * NLO + zl1, c1))
+        for d in (1, 2, 0):
+            zl1 = (zl + d) % NLO
+            for e in range(2):
+                tile = xbuf[group[k] * NLO + zl1, e]
+                new = jnp.dot(high, tile, preferred_element_type=jnp.float32)
+                new += jnp.dot(low, tile, preferred_element_type=jnp.float32)
+                new = new.reshape(NX, J, T)
+                op[d, :, e] = new if k == 0 else op[d, :, e] + new
+            if k == NHI - 1:
+                for i in (2, 1, 3):
+                    x1 = (x + i) % NX
+                    copy(op.at[d, x1], rx.at[d, i - 1], p4r.at[d, i - 1], dev(x1, y, z, c))
+    for d in (1, 2, 0):
+        zl1 = (zl + d) % NLO
+        total = op[d, x]
+        for i in (1, 3, 2):
+            arrived(rx.at[d, i - 1], p4r.at[d, i - 1])
+            total += rx[d, i - 1]
+        fsum[d] = total
+        for e in range(2):
+            c1 = (c + e) % 2
+            if d or e:
+                copy(fsum.at[d, c1], fin.at[c, zl], p5r.at[d, e], dev(x, y, zh * NLO + zl1, c1))
+            else:
+                fin[c, zl] = fsum[d, c]
+    hops = [(d, e) for d in (0, 1, 2) for e in range(2) if d or e]
     tot = dgs2[...]
     for d in range(1, NHI):
         arrived(dgz.at[d - 1], dzr.at[d - 1])
@@ -241,7 +254,7 @@
     scale = 2.0 * weight_off / images
     for d, e in hops:
         arrived(fin.at[(c + e) % 2, (zl + NLO - d) % NLO], p5r.at[d, e])
-    for t, (out, other) in enumerate(((ga_ref, b_ref), (gb_ref, a_ref))):
+    for t, (out, other) in enumerate(((ga_ref, own.at[1]), (gb_ref, own.at[0]))):
         for i, rows in enumerate((J, J, T - 2 * J)):
             at = pl.ds(i * J, rows)
             gram_term = fin[t, i, pl.ds(J - rows, rows), :]
@@ -255,11 +268,12 @@
     f32, bf16 = jnp.float32, jnp.bfloat16
     dma = pltpu.SemaphoreType.DMA
     vmem = pl.BlockSpec(memory_space=pltpu.VMEM)
+    hbm = pl.BlockSpec(memory_space=pl.ANY)
     smem = pl.BlockSpec(memory_space=pltpu.SMEM)
     return pl.pallas_call(
         functools.partial(kernel, float(images)),
         out_shape=[jax.ShapeDtypeStruct((T, T), f32)] * 2,
-        in_specs=[smem, smem, vmem, vmem],
+        in_specs=[smem, smem, hbm, hbm],
         out_specs=[vmem, vmem],
         scratch_shapes=[
             pltpu.VMEM((2, T, T), bf16),
@@ -269,27 +283,30 @@
             pltpu.VMEM((NHI, NY - 1, PY, T), f32),
             pltpu.VMEM((NHI, PY, T), f32),
             pltpu.VMEM((NHI, JR, T), f32),
-            pltpu.VMEM((NLO * 2, NX, J, T), f32),
-            pltpu.VMEM((NX - 1, NLO * 2, J, T), f32),
-            pltpu.VMEM((NLO * 2, J, T), f32),
+            pltpu.VMEM((NLO, NX, 2, J, T), f32),
+            pltpu.VMEM((NLO, NX - 1, 2, J, T), f32),
+            pltpu.VMEM((NLO, 2, J, T), f32),
             pltpu.VMEM((2, NLO, J, T), f32),
             pltpu.VMEM((8, T), f32),
             pltpu.VMEM((NX - 1, 8, T), f32),
             pltpu.VMEM((8, T), f32),
             pltpu.VMEM((NHI - 1, 8, T), f32),
-            dma((104,)),
-            dma((2, 6, 2)),
+            dma((112,)),
+            dma((2,)),
+            pltpu.SemaphoreType.REGULAR,
+            pltpu.SemaphoreType.REGULAR((NY // 2 - 1, 2)),
+            dma((2, 12)),
             dma((1,)),
             dma((NX - 1,)),
             dma((NHI, NY - 1)),
             dma((NHI, NY)),
-            dma((NX - 1,)),
+            dma((NLO, NX - 1)),
             dma((NLO, 2)),
             dma((NX - 1,)),
             dma((NHI - 1,)),
         ],
         compiler_params=pltpu.CompilerParams(
-            collective_id=0, has_side_effects=True, vmem_limit_bytes=32 << 20
+            collective_id=0, has_side_effects=True, vmem_limit_bytes=60 << 20
         ),
         name="gram_grads",
     )(weight_off.reshape(1), loss_grad.reshape(1), view_a, view_b)

time: 70.4 us -> 67.4 us (0.957)
  the two profiles are of different devices: /device:TPU:3 before, /device:TPU:1 now
where the time goes in v3:
time: 67.4 us; the launch traced here: 67.1 us
  Pallas kernels  63.1 us (94%)
  local copies, waits for them, and re-layouts  2.14 us (3%)
  between operations  1.94 us (3%)
    pallas_call x1, Pallas kernels, local(): pl.pallas_call(functools.partial(kernel, float(images)), out_shape=[jax.S...  63.1 us
    unnamed x4, local copies, waits for them, and re-layouts  2.14 us

profile of v3, /device:TPU:1, one launch (start us, length us, event | category | flops | bytes accessed | tf_op | source)
XLA Modules:
  0.0 67.1 jit_solution(7909117607067813364)
XLA Ops:
  1.9 63.1 %gram_grads.1 = (f32[128,128]{1,0:T(8,128)}, f32[128,128]{1,0:T(8,128)}) custom-call(f32[1]{0:T(128)} %bitcast.2.w_ref, f32[1]{0:T(128)} %bitcast.3.l_ref, bf16[128,128]{1,0:T(8,128)(2,1)} %a_ref.1, bf16[128,128]{1,0:T(8,128)(2,1)} %b_ref.1), custom_call_target="tpu_custom_call" | custom-call | tf_op jit(solution)/shard_map/gram_grads/pallas_call | solution.py:273
  65.0 0.0 copy-start
  65.0 1.5 %copy.10 = f32[128,128]{1,0:T(8,128)} copy(f32[128,128]{1,0:T(8,128)} %get-tuple-element.4) | data formatting | bytes 131072
  66.5 0.0 copy-done
  66.5 0.6 copy.11
Async XLA Ops:
  65.0 1.5 %copy-start = (f32[128,128]{1,0:T(8,128)S(1)}, f32[128,128]{1,0:T(8,128)}, u32[]{:S(2)}) copy-start(f32[128,128]{1,0:T(8,128)} %get-tuple-element.5) | copy-start | bytes 196612

commit v4 on v3

--- a/solution.py
+++ b/solution.py
@@ -26,11 +26,9 @@
 def kernel(
     images,
     w_ref,
-    l_ref,
     a_ref,
     b_ref,
-    ga_ref,
-    gb_ref,
+    g_ref,
     own,
     xbuf,
     xj,
@@ -119,6 +117,9 @@
         if t == 0:
             pl.semaphore_signal(xin, inc=1, device_id=dev(xl, y, z, c), device_id_type=MESH)
             copy(own.at[1 - c], xbuf.at[z, c], sibr.at[0], dev(x, y, z, 1 - c))
+            n_first = 4
+            for cp in sent[:n_first]:
+                cp.wait_send()
     for n in range(NY // 2 - 1):
         for i, yn in enumerate((yr, yl)):
             pl.semaphore_signal(yin.at[n, i], inc=1, device_id=dev(x, yn, z, c), device_id_type=MESH)
@@ -249,17 +250,17 @@
         arrived(dgz.at[d - 1], dzr.at[d - 1])
         tot += dgz[d - 1]
     weight_off = w_ref[0]
-    loss_grad = l_ref[0]
     shift = -2.0 + (2.0 * (1.0 - weight_off) / images) * jnp.sum(tot, axis=0, keepdims=True)
     scale = 2.0 * weight_off / images
     for d, e in hops:
         arrived(fin.at[(c + e) % 2, (zl + NLO - d) % NLO], p5r.at[d, e])
-    for t, (out, other) in enumerate(((ga_ref, own.at[1]), (gb_ref, own.at[0]))):
+    for t in range(2):
+        other = own.at[1 - t]
         for i, rows in enumerate((J, J, T - 2 * J)):
             at = pl.ds(i * J, rows)
             gram_term = fin[t, i, pl.ds(J - rows, rows), :]
-            out[at, :] = loss_grad * (scale * gram_term + other[at, :].astype(jnp.float32) * shift)
-    for cp in sent:
+            g_ref[t, at, :] = scale * gram_term + other[at, :].astype(jnp.float32) * shift
+    for cp in sent[n_first:]:
         cp.wait_send()
 
 
@@ -270,11 +271,11 @@
     vmem = pl.BlockSpec(memory_space=pltpu.VMEM)
     hbm = pl.BlockSpec(memory_space=pl.ANY)
     smem = pl.BlockSpec(memory_space=pltpu.SMEM)
-    return pl.pallas_call(
+    grads = pl.pallas_call(
         functools.partial(kernel, float(images)),
-        out_shape=[jax.ShapeDtypeStruct((T, T), f32)] * 2,
-        in_specs=[smem, smem, hbm, hbm],
-        out_specs=[vmem, vmem],
+        out_shape=jax.ShapeDtypeStruct((2, T, T), f32),
+        in_specs=[smem, hbm, hbm],
+        out_specs=vmem,
         scratch_shapes=[
             pltpu.VMEM((2, T, T), bf16),
             pltpu.VMEM((NZ, 2, T, T), bf16),
@@ -309,7 +310,8 @@
             collective_id=0, has_side_effects=True, vmem_limit_bytes=60 << 20
         ),
         name="gram_grads",
-    )(weight_off.reshape(1), loss_grad.reshape(1), view_a, view_b)
+    )(weight_off.reshape(1), view_a, view_b)
+    return loss_grad * grads[0], loss_grad * grads[1]
 
 
 def solution(mesh):

time: 67.4 us -> 64.5 us (0.957)
  Pallas kernels: 63.1 us -> 60.8 us
  local copies, waits for them, and re-layouts: 2.14 us -> 0 us
  other arithmetic: 0 us -> 1.53 us
    pallas_call x1, Pallas kernels: 63.1 us -> 60.8 us  [local(): pl.pallas_call(functools.partial(kernel, float(images)), out_shape=jax.Sh...]
    unnamed x4 -> x0, local copies, waits for them, and re-layouts: 2.14 us -> none
    mul x0 -> x1, other arithmetic: none -> 1.53 us  [local(): return (loss_grad * grads[0], loss_grad * grads[1])]
where the time goes in v4:
time: 64.5 us; the launch traced here: 64.2 us
  Pallas kernels  60.8 us (94%)
  between operations  1.93 us (3%)
  other arithmetic  1.53 us (2%)
    pallas_call x1, Pallas kernels, local(): pl.pallas_call(functools.partial(kernel, float(images)), out_shape=jax.Sh...  60.8 us
    mul x1, other arithmetic, local(): return (loss_grad * grads[0], loss_grad * grads[1])  1.53 us

profile of v4, /device:TPU:1, one launch (start us, length us, event | category | flops | bytes accessed | tf_op | source)
XLA Modules:
  0.0 64.2 jit_solution(9128145896523095129)
XLA Ops:
  1.9 60.8 %gram_grads.1 = f32[2,128,128]{2,1,0:T(8,128)} custom-call(f32[1]{0:T(128)} %bitcast.5.w_ref, bf16[128,128]{1,0:T(8,128)(2,1)} %a_ref.1, bf16[128,128]{1,0:T(8,128)(2,1)} %b_ref.1), custom_call_target="tpu_custom_call" | custom-call | tf_op jit(solution)/shard_map/gram_grads/pallas_call | solution.py:274
  62.7 1.5 %multiply_bitcast_fusion = (f32[128,128]{1,0:T(8,128)}, f32[128,128]{1,0:T(8,128)}) fusion(f32[2,128,128]{2,1,0:T(8,128)} %gram_grads.1, f32[]{:T(128)S(6)} %copy.7), kind=kLoop, calls=%fused_computation | loop fusion | flops 32768 | bytes 262148 | tf_op jit(solution)/shard_map/mul | solution.py:314

commit v5 on v4

--- a/solution.py
+++ b/solution.py
@@ -14,7 +14,7 @@
 J = 48
 JR = NX * J
 PY = JR // NY
-TREE = {2: 0, -2: 0, 1: 0, -1: 0, 4: 2, -4: -2, 3: 2, -3: -2, 5: 4, -5: -4, 6: 4}
+TREE = {1: 0, -1: 0, 2: 1, -2: -1, 3: 2, -3: -2, 4: 3, -4: -3, 5: 4, -5: -4, 6: 5}
 NEXT = {p: [d for d in TREE if TREE[d] == p] for p in (0, *TREE)}
 FAR = max(abs(d) for d in NEXT[0])
 
@@ -26,10 +26,8 @@
 def kernel(
     images,
     w_ref,
-    a_ref,
-    b_ref,
+    own,
     g_ref,
-    own,
     xbuf,
     xj,
     part,
@@ -45,7 +43,6 @@
     dgs2,
     dgz,
     ssem,
-    loaded,
     xin,
     yin,
     p1r,
@@ -76,13 +73,6 @@
     peers += [dev(x, y, at_z(s * d), t) for d in range(1, FAR + 1) for s in (1, -1) for t in range(2)]
     for p in peers:
         pl.semaphore_signal(bar, inc=1, device_id=p, device_id_type=MESH)
-    loads = [
-        pltpu.make_async_copy(ref, own.at[t], loaded.at[t]) for t, ref in enumerate((a_ref, b_ref))
-    ]
-    for cp in loads:
-        cp.start()
-    for cp in loads:
-        cp.wait()
     xbuf[z, c] = own[c]
     pl.semaphore_wait(bar, len(peers))
 
@@ -117,9 +107,6 @@
         if t == 0:
             pl.semaphore_signal(xin, inc=1, device_id=dev(xl, y, z, c), device_id_type=MESH)
             copy(own.at[1 - c], xbuf.at[z, c], sibr.at[0], dev(x, y, z, 1 - c))
-            n_first = 4
-            for cp in sent[:n_first]:
-                cp.wait_send()
     for n in range(NY // 2 - 1):
         for i, yn in enumerate((yr, yl)):
             pl.semaphore_signal(yin.at[n, i], inc=1, device_id=dev(x, yn, z, c), device_id_type=MESH)
@@ -194,10 +181,12 @@
                 copy(xbuf.at[zc, j], xbuf.at[zc, j], p1r.at[j, e + 5], dev(x, y, at_z(s * (e - d)), c))
         if d == -1:
             arrived(xbuf.at[z, 1 - c], sibr.at[0])
+        if d == -2:
             send_j()
         if d == -3:
             wait_j()
             gram(0)
+        if d == -4:
             gram(1)
         if d == -5:
             gram(2)
@@ -260,7 +249,7 @@
             at = pl.ds(i * J, rows)
             gram_term = fin[t, i, pl.ds(J - rows, rows), :]
             g_ref[t, at, :] = scale * gram_term + other[at, :].astype(jnp.float32) * shift
-    for cp in sent[n_first:]:
+    for cp in sent:
         cp.wait_send()
 
 
@@ -269,15 +258,13 @@
     f32, bf16 = jnp.float32, jnp.bfloat16
     dma = pltpu.SemaphoreType.DMA
     vmem = pl.BlockSpec(memory_space=pltpu.VMEM)
-    hbm = pl.BlockSpec(memory_space=pl.ANY)
     smem = pl.BlockSpec(memory_space=pltpu.SMEM)
     grads = pl.pallas_call(
         functools.partial(kernel, float(images)),
         out_shape=jax.ShapeDtypeStruct((2, T, T), f32),
-        in_specs=[smem, hbm, hbm],
+        in_specs=[smem, vmem],
         out_specs=vmem,
         scratch_shapes=[
-            pltpu.VMEM((2, T, T), bf16),
             pltpu.VMEM((NZ, 2, T, T), bf16),
             pltpu.VMEM((NLO, 2, NX, J, T), bf16),
             pltpu.VMEM((NHI, JR, T), f32),
@@ -293,7 +280,6 @@
             pltpu.VMEM((8, T), f32),
             pltpu.VMEM((NHI - 1, 8, T), f32),
             dma((112,)),
-            dma((2,)),
             pltpu.SemaphoreType.REGULAR,
             pltpu.SemaphoreType.REGULAR((NY // 2 - 1, 2)),
             dma((2, 12)),
@@ -307,10 +293,10 @@
             dma((NHI - 1,)),
         ],
         compiler_params=pltpu.CompilerParams(
-            collective_id=0, has_side_effects=True, vmem_limit_bytes=60 << 20
+            collective_id=0, has_side_effects=True, vmem_limit_bytes=32 << 20
         ),
         name="gram_grads",
-    )(weight_off.reshape(1), view_a, view_b)
+    )(weight_off.reshape(1), jnp.stack([view_a, view_b]))
     return loss_grad * grads[0], loss_grad * grads[1]
 
 

time: 64.5 us -> 63.1 us (0.978)
  Pallas kernels: 60.8 us -> 59.5 us
    pallas_call x1, Pallas kernels: 60.8 us -> 59.5 us  [local(): pl.pallas_call(functools.partial(kernel, float(images)), out_shape=jax.Sh...]
    mul x1, other arithmetic: 1.53 us -> 0.66 us  [local(): return (loss_grad * grads[0], loss_grad * grads[1])]
    another operation x0 -> x1, other arithmetic: none -> 0.78 us  [local(): jnp.stack([view_a, view_b])]
where the time goes in v5:
time: 63.1 us; the launch traced here: 62.9 us
  Pallas kernels  59.5 us (94%)
  between operations  1.93 us (3%)
  other arithmetic  1.44 us (2%)
    pallas_call x1, Pallas kernels, local(): pl.pallas_call(functools.partial(kernel, float(images)), out_shape=jax.Sh...  59.5 us

profile of v5, /device:TPU:1, one launch (start us, length us, event | category | flops | bytes accessed | tf_op | source)
XLA Modules:
  0.0 62.9 jit_solution(2801276125227091414)
XLA Ops:
  1.9 0.8 %pad_maximum_fusion.own = bf16[2,128,128]{2,1,0:T(8,128)(2,1)S(1)} fusion(bf16[1,128,128]{2,1,0:T(8,128)(2,1)} %bitcast.8, bf16[1,128,128]{2,1,0:T(8,128)(2,1)} %bitcast.9), kind=kLoop, calls=%fused_computation | loop fusion | flops 32768 | bytes 131072 | tf_op jit(solution)/shard_map/stack | solution.py:299
  2.7 59.5 %gram_grads.1 = f32[2,128,128]{2,1,0:T(8,128)S(1)} custom-call(f32[1]{0:T(128)} %bitcast.7.w_ref, bf16[2,128,128]{2,1,0:T(8,128)(2,1)S(1)} %pad_maximum_fusion.own), custom_call_target="tpu_custom_call" | custom-call | tf_op jit(solution)/shard_map/gram_grads/pallas_call | solution.py:262
  62.2 0.7 %multiply_bitcast_fusion = (f32[128,128]{1,0:T(8,128)}, f32[128,128]{1,0:T(8,128)}) fusion(f32[2,128,128]{2,1,0:T(8,128)S(1)} %gram_grads.1, f32[]{:T(128)S(6)} %copy.7), kind=kLoop, calls=%fused_computation.1 | loop fusion | flops 32768 | bytes 262148 | tf_op jit(solution)/shard_map/mul | solution.py:300

commit v6 on v5

--- a/solution.py
+++ b/solution.py
@@ -191,6 +191,9 @@
         if d == -5:
             gram(2)
     gram(3)
+    for k in range(NHI):
+        reduce(k)
+
     tot = dgs[...]
     for d in range(1, NX):
         arrived(dgx.at[d - 1], dxr.at[d - 1])
@@ -198,9 +201,6 @@
     dgs2[...] = tot
     for d in range(1, NHI):
         copy(dgs2, dgz.at[d - 1], dzr.at[d - 1], dev(x, y, (z + NLO * d) % NZ, c))
-    for k in range(NHI):
-        reduce(k)
-
     for k in range(NHI):
         for d in range(NY):
             y1 = (y + NY - d) % NY

time: 63.1 us -> 63 us (level)
  no operation moved by 1% of the time
where the time goes in v6:
time: 63 us; the launch traced here: 62.8 us
  Pallas kernels  59.4 us (94%)
  between operations  1.93 us (3%)
  other arithmetic  1.44 us (2%)
    pallas_call x1, Pallas kernels, local(): pl.pallas_call(functools.partial(kernel, float(images)), out_shape=jax.Sh...  59.4 us

profile of v6, /device:TPU:1, one launch (start us, length us, event | category | flops | bytes accessed | tf_op | source)
XLA Modules:
  0.0 62.8 jit_solution(9723566047098218129)
XLA Ops:
  1.9 0.8 %pad_maximum_fusion.own = bf16[2,128,128]{2,1,0:T(8,128)(2,1)S(1)} fusion(bf16[1,128,128]{2,1,0:T(8,128)(2,1)} %bitcast.8, bf16[1,128,128]{2,1,0:T(8,128)(2,1)} %bitcast.9), kind=kLoop, calls=%fused_computation | loop fusion | flops 32768 | bytes 131072 | tf_op jit(solution)/shard_map/stack | solution.py:299
  2.7 59.4 %gram_grads.1 = f32[2,128,128]{2,1,0:T(8,128)S(1)} custom-call(f32[1]{0:T(128)} %bitcast.7.w_ref, bf16[2,128,128]{2,1,0:T(8,128)(2,1)S(1)} %pad_maximum_fusion.own), custom_call_target="tpu_custom_call" | custom-call | tf_op jit(solution)/shard_map/gram_grads/pallas_call | solution.py:262
  62.1 0.7 %multiply_bitcast_fusion = (f32[128,128]{1,0:T(8,128)}, f32[128,128]{1,0:T(8,128)}) fusion(f32[2,128,128]{2,1,0:T(8,128)S(1)} %gram_grads.1, f32[]{:T(128)S(6)} %copy.7), kind=kLoop, calls=%fused_computation.1 | loop fusion | flops 32768 | bytes 262148 | tf_op jit(solution)/shard_map/mul | solution.py:300
